TPU v7x, 32 devices: a whole 2x2x4 slice. The times are simulated.
32 devices in a mesh: wind: 2 (over y), gx: 4 (over z), gy: 2 (over x), gz: 2 (over core).
Axes of the slice: x: 2, y: 2, z: 4, core: 2. Of those that a mesh axis runs over, the one named last changes fastest.
Arguments:
- pressure: bfloat16 [8192, 8192], P(('wind', 'gx'), ('gy', 'gz')), parts along dimension 0, may hold values from -40 to 40
- fir_taps: bfloat16 [257], replicated, may hold values from -0.375 to 0.375
- influence: bfloat16 [256, 4, 4, 512], P(None, ('gy', 'gz'), 'gx'), may hold values from -0.0625 to 0.0625
- mode_impulse: float32 [256, 64], replicated, may hold values from -0.75 to 0.75
- mode_taps: int32 [256], replicated, may hold values from 1 to 64, as said below
Outputs:
- responses: bfloat16 [512, 4096], P(('wind', 'gx', 'gy', 'gz')), parts along dimension 0
- correlation_score: float32 [512, 4, 4, 512], P('wind', ('gy', 'gz'), 'gx'), parts along dimension 0
There are 2 independent parts, one for each index of `wind`. A program takes and returns all parts, laid end to end along the dimension named above; an argument that names none is the same for every part. Nothing has to cross between parts.
Inputs may be any that keep to these rules, and one draw needn't show every extreme that they name: `mode_taps`: some mode keeps all 64 taps.
All inputs are finite; a program needn't handle non-finite values.
Results may differ from a plain program's by a relative error of at most 0.005.
Values may be sent and summed in bfloat16 or wider, within the bound.
A program may use at most 64 MiB of HBM per device.

v0:
```python
import math

import jax
import jax.numpy as jnp
from jax import lax
from jax.sharding import PartitionSpec as P


def band_matrix(tap_row, row_count):
    tap_count = tap_row.shape[0]
    extended = jnp.concatenate([tap_row[::-1], jnp.zeros((row_count,), tap_row.dtype)])
    tiled_flat = jnp.tile(extended, row_count)[: row_count * (row_count + tap_count - 1)]
    return tiled_flat.reshape(row_count, row_count + tap_count - 1)


def fir_rows(padded_in, tap_row, row_count):
    tap_count = tap_row.shape[0]
    block_rows = min(512, row_count)
    toeplitz = band_matrix(tap_row, block_rows)
    partials = [
        jnp.dot(
            toeplitz,
            padded_in[offset : offset + block_rows + tap_count - 1],
            preferred_element_type=jnp.float32,
        )
        for offset in range(0, row_count, block_rows)
    ]
    return jnp.concatenate(partials, axis=0).astype(jnp.bfloat16)


def dynamic_filter(series, impulse, tap_limits):
    impulse_len = impulse.shape[1]
    kept_mask = jnp.arange(impulse_len, dtype=jnp.int32)[None, :] < tap_limits[:, None]
    kernel_taps = jnp.where(kept_mask, impulse, jnp.zeros_like(impulse))[:, ::-1]
    result = lax.conv_general_dilated(
        series[None],
        kernel_taps[:, None, :],
        window_strides=(1,),
        padding=[(impulse_len - 1, 0)],
        dimension_numbers=("NCH", "OIH", "NCH"),
        feature_group_count=series.shape[0],
        precision=lax.Precision.HIGHEST,
    )
    return result[0]


def score_block(responses, filtered, mean_panel, spread_panel):
    sample_count = filtered.shape[0]
    resp_wide = responses.astype(jnp.float32)
    mean_mode = jnp.mean(resp_wide, axis=1)
    spread_mode = jnp.sqrt(jnp.mean(jnp.square(resp_wide - mean_mode[:, None]), axis=1) + 1e-06)
    cross = jnp.dot(responses, filtered, preferred_element_type=jnp.float32)
    covariance = cross / sample_count - mean_mode[:, None] * mean_panel[None, :]
    return math.sqrt(sample_count) * covariance / (spread_mode[:, None] * spread_panel[None, :])


def body(pressure, fir_taps, influence, mode_impulse, mode_taps):
    tap_count = fir_taps.shape[0]
    regrouped = lax.all_to_all(pressure, "gx", split_axis=1, concat_axis=0, tiled=True)
    zero_rim = jnp.zeros((tap_count - 1, regrouped.shape[1]), regrouped.dtype)
    filtered = fir_rows(
        jnp.concatenate([zero_rim, regrouped], axis=0), fir_taps, regrouped.shape[0]
    )
    lines = influence.reshape(influence.shape[0], -1)
    mode_count = lines.shape[0]
    per_device = mode_count // lax.axis_size(("gx", "gy", "gz"))
    mean_panel = jnp.mean(filtered, axis=0, dtype=jnp.float32)
    spread_panel = jnp.sqrt(
        jnp.mean(jnp.square(filtered.astype(jnp.float32) - mean_panel[None, :]), axis=0) + 1e-06
    )
    first_mode = lax.axis_index(("gx", "gy", "gz")) * per_device
    own_loads = lax.psum_scatter(
        lax.dot_general(
            lines, filtered, (((1,), (1,)), ((), ())), preferred_element_type=jnp.float32
        ),
        ("gx", "gy", "gz"),
        scatter_dimension=0,
        tiled=True,
    )
    own_impulse = lax.dynamic_slice_in_dim(mode_impulse, first_mode, per_device, 0)
    own_limits = lax.dynamic_slice_in_dim(mode_taps, first_mode, per_device, 0)
    own_modes = dynamic_filter(own_loads, own_impulse, own_limits).astype(jnp.bfloat16)
    scores = score_block(
        lax.all_gather(own_modes, ("gx", "gy", "gz"), axis=0, tiled=True),
        filtered,
        mean_panel,
        spread_panel,
    )
    return (own_modes, scores.reshape(influence.shape))


def solution(mesh):
    return jax.shard_map(
        body,
        mesh=mesh,
        in_specs=(
            P(("wind", "gx"), ("gy", "gz")),
            P(),
            P(None, ("gy", "gz"), "gx", None),
            P(),
            P(),
        ),
        out_specs=(P(("wind", "gx", "gy", "gz"), None), P("wind", ("gy", "gz"), "gx", None)),
        check_vma=False,
    )
```

profile of v0, /device:TPU:0, one launch (start us, length us, event | category | flops | bytes accessed | tf_op | source)
XLA Modules:
  0.0 279.5 jit_solution(2012428702665789185)
XLA Ops:
  7.2 6.5 %copy.44 = bf16[1024,2048]{0,1:T(8,128)(2,1)} copy(bf16[1024,2048]{1,0:T(8,128)(2,1)} %param.5) | data formatting | bytes 8388608 | tf_op args[0]
  13.7 6.4 %all-to-all-start = ((bf16[1024,4,512]{0,2,1:T(8,128)(2,1)}), bf16[1024,4,512]{0,2,1:T(8,128)(2,1)}, u32[]{:S(2)}, u32[]{:S(2)}) async-start(bf16[1024,4,512]{0,2,1:T(8,128)(2,1)} %bitcast.53), calls=%async_computation | async-start | bytes 8388608 | tf_op jit(solution)/shard_map/all_to_all | solution.py:59
  20.4 1.3 tile.10
  21.8 0.7 reshape.35
  22.5 91.1 %all-to-all-done = bf16[1024,4,512]{0,2,1:T(8,128)(2,1)} async-done(((bf16[1024,4,512]{0,2,1:T(8,128)(2,1)}), bf16[1024,4,512]{0,2,1:T(8,128)(2,1)}, u32[]{:S(2)}, u32[]{:S(2)}) %all-to-all-start) | async-done | bytes 4194336 | tf_op jit(solution)/shard_map/all_to_all | solution.py:59
  113.6 6.2 %copy.45 = bf16[4,1024,512]{2,1,0:T(8,128)(2,1)} copy(bf16[4,1024,512]{1,2,0:T(8,128)(2,1)} %bitcast.1) | data formatting | bytes 8388608 | tf_op jit(solution)/shard_map/all_to_all | solution.py:59
  119.8 1.7 fusion.18
  121.5 0.6 copy-done.4
  123.3 0.6 fusion.15
  126.2 1.9 copy-done.1
  128.1 3.2 %convolution_bitcast_fusion = f32[256,4096]{0,1:T(8,128)} fusion(bf16[4096,512]{1,0:T(8,128)(2,1)S(1)} %fusion.11, bf16[256,1,1,512]{3,0,2,1:T(8,128)(2,1)S(1)} %copy-done), kind=kOutput, calls=%fused_computation.4 | convolution fusion | flops 1073741824 | bytes 8650752 | tf_op jit(solution)/shard_map/dot_general | solution.py:73
  131.3 5.6 %copy.56 = f32[256,4096]{1,0:T(8,128)} copy(f32[256,4096]{0,1:T(8,128)} %convolution_bitcast_fusion) | data formatting | bytes 8388608
  137.9 70.8 %reduce-scatter.4.cloned.1.call-done = f32[16,4096]{1,0:T(8,128)} async-done(((f32[256,4096]{1,0:T(8,128)}), f32[16,4096]{1,0:T(8,128)}) %reduce-scatter.4.cloned.1.call-update) | async-done | bytes 262160
  208.7 1.5 copy.57
  211.0 10.8 %fusion.5 = bf16[8,520,16]{2,0,1:T(8,128)(2,1)S(1)} fusion(f32[16,1,64]{0,1,2:T(1,128)S(1)} %bitcast.64, f32[16,1,7,63]{0,2,3,1:T(8,128)S(1)} %slice.46, f32[16,1,8,520]{0,2,3,1:T(8,128)S(1)} %copy.48), kind=kOutput, calls=%fused_computation.12 | convolution fusion | flops 51341952 | bytes 431680 | tf_op jit(solution)/shard_map/conv_general_dilated | solution.py:35
  221.7 0.7 copy.50
  222.7 0.7 slice_bitcast_fusion.1
  223.5 3.0 %convert_reduce_fusion = f32[512]{0:T(512)S(1)} fusion(bf16[4096,512]{1,0:T(8,128)(2,1)} %copy-done.1), kind=kLoop, calls=%fused_computation.1 | loop fusion | flops 4193792 | bytes 4196352 | tf_op jit(solution)/shard_map/reduce_sum | solution.py:67
  226.9 1.2 fusion.1
  228.1 35.9 %all-gather.3.cloned.1.call-done = bf16[1,256,4096]{2,1,0:T(8,128)(2,1)} async-done(((bf16[1,16,4096]{2,1,0:T(8,128)(2,1)}), bf16[1,256,4096]{2,1,0:T(8,128)(2,1)}) %all-gather.3.cloned.1.call-update) | async-done | bytes 2097168 | tf_op jit(solution)/shard_map/all_gather | solution.py:84
  264.0 2.1 convert_reduce_fusion.1
  266.1 2.3 fusion.3
  268.4 2.9 %fusion.33 = f32[256,1,1,512]{3,0,2,1:T(8,128)S(1)} fusion(bf16[4096,512]{1,0:T(8,128)(2,1)S(1)} %copy-done.3, bf16[1,256,4096]{2,1,0:T(8,128)(2,1)} %all-gather.3.cloned.1.call-done, f32[512]{0:T(512)S(1)} %add_sqrt_fusion, f32[256]{0:T(256)S(1)} %add_sqrt_fusion.1, f32[512]{0:T(512)S(1)} %broadcast_multiply_fusion, f32[256]{0:T(256)S(1)} %broadcast_multiply_fusion.1), kind=kOutput, calls=%fused_computation.40 | convolution fusion | flops 1074528256 | bytes 6821888 | tf_op jit(solution)/shard_map/dot_general | solution.py:52
  271.3 1.3 copy.52
  (44 shorter events, 6.1 us)
Async XLA Ops:
  7.2 120.9 %copy-start = (bf16[256,1,1,512]{3,0,2,1:T(8,128)(2,1)S(1)}, bf16[256,1,1,512]{3,0,2,1:T(8,128)(2,1)}, u32[]{:S(2)}) copy-start(bf16[256,1,1,512]{3,0,2,1:T(8,128)(2,1)} %param.7) | copy-start | bytes 786436
  13.7 6.5 %copy-start.7 = (bf16[257]{0:T(512)(128)(2,1)S(1)}, bf16[257]{0:T(512)(128)(2,1)}, u32[]{:S(2)}) copy-start(bf16[257]{0:T(512)(128)(2,1)} %param.6) | copy-start | bytes 1546
  13.7 99.9 %all-to-all-start = ((bf16[1024,4,512]{0,2,1:T(8,128)(2,1)}), bf16[1024,4,512]{0,2,1:T(8,128)(2,1)}, u32[]{:S(2)}, u32[]{:S(2)}) async-start(bf16[1024,4,512]{0,2,1:T(8,128)(2,1)} %bitcast.53), calls=%async_computation | async-start | bytes 8388608 | tf_op jit(solution)/shard_map/all_to_all | solution.py:59
  20.1 188.6 %reduce-scatter.4.cloned.1.call-start = ((), (), s32[]{:S(2)}) async-start(), calls=%async_computation.3 | async-start | bytes 4456448
  119.8 2.3 copy-start.4
  126.2 1.9 copy-start.1
  137.0 0.7 copy-start.8
  137.0 0.9 copy-start.5
  137.0 127.0 %all-gather.3.cloned.1.call-start = ((), (), s32[]{:S(2)}) async-start(), calls=%async_computation.2 | async-start | bytes 2228224 | tf_op jit(solution)/shard_map/all_gather | solution.py:84
  210.9 11.5 %copy-start.6 = (pred[8,520]{1,0:T(8,128)(4,1)S(1)}, pred[8,520]{1,0:T(8,128)(4,1)}, u32[]{:S(2)}) copy-start(pred[8,520]{1,0:T(8,128)(4,1)} %constant.52) | copy-start | bytes 12484
  223.4 3.5 %copy-start.2 = (bf16[4096,512]{1,0:T(8,128)(2,1)S(1)}, bf16[4096,512]{1,0:T(8,128)(2,1)}, u32[]{:S(2)}) copy-start(bf16[4096,512]{1,0:T(8,128)(2,1)} %copy-done.1) | copy-start | bytes 12582916
  264.0 4.4 %copy-start.3 = (bf16[4096,512]{1,0:T(8,128)(2,1)S(1)}, bf16[4096,512]{1,0:T(8,128)(2,1)}, u32[]{:S(2)}) copy-start(bf16[4096,512]{1,0:T(8,128)(2,1)} %copy-done.1) | copy-start | bytes 12582916
Sparse Core Ops, SparseCore 0:
  137.1 71.5 reduce-scatter.3
  223.6 40.3 all-gather.2
where the time goes:
time: 280 us
  waiting for transfers between devices  198 us (71%)
  local copies, waits for them, and re-layouts  29.5 us (11%)
  matrix products  22.6 us (8%)
  between operations  14.2 us (5%)
  other arithmetic  8.64 us (3%)
  starting transfers between devices  6.67 us (2%)
    all_to_all x1, waiting for transfers between devices, body(): lax.all_to_all(pressure, 'gx', split_axis=1, concat_axis=0, tiled=True)  91.1 us
    unnamed x3, waiting for transfers between devices  70.8 us
    all_gather x1, waiting for transfers between devices, body(): lax.all_gather(own_modes, ('gx', 'gy', 'gz'), axis=0, tiled=True)  35.9 us
    unnamed x24, local copies, waits for them, and re-layouts  18.8 us
    conv_general_dilated x1, matrix products, dynamic_filter(): lax.conv_general_dilated(series[None], kernel_taps[:, None, :], window_st...  10.8 us
    all_to_all x1, starting transfers between devices, body(): lax.all_to_all(pressure, 'gx', split_axis=1, concat_axis=0, tiled=True)  6.45 us
    all_to_all x1, local copies, waits for them, and re-layouts, body(): lax.all_to_all(pressure, 'gx', split_axis=1, concat_axis=0, tiled=True)  6.23 us
    dot_general x8, matrix products, fir_rows(): jnp.dot(toeplitz, padded_in[offset:offset + block_rows + tap_count - 1],...  5.71 us
  transfers between devices with their start and end apart: 3, of which 3 were waited for; matrix products, arithmetic and copies ran while one was open for 2% of the time, Pallas kernels for 0%

commit v1 on v0

v1 whole, which is shorter than its diff:
```python
import math

import jax
import jax.numpy as jnp
from jax import lax
from jax.sharding import PartitionSpec as P

F32 = jnp.float32
BF16 = jnp.bfloat16


def dot(a, b, contract):
    return lax.dot_general(a, b, (contract, ((), ())), preferred_element_type=F32)


def band_matrix(tap_row, row_count):
    tap_count = tap_row.shape[0]
    extended = jnp.concatenate([tap_row, jnp.zeros((row_count,), tap_row.dtype)])
    flat = jnp.tile(extended, row_count)[: row_count * (row_count + tap_count - 1)]
    return flat.reshape(row_count, row_count + tap_count - 1)


def windows(padded, block, width):
    count = (padded.shape[1] - (width - block)) // block
    return jnp.stack([padded[:, i * block : i * block + width] for i in range(count)], axis=1)


def dynamic_filter(series, impulse, tap_limits):
    impulse_len = impulse.shape[1]
    kept_mask = jnp.arange(impulse_len, dtype=jnp.int32)[None, :] < tap_limits[:, None]
    kernel_taps = jnp.where(kept_mask, impulse, jnp.zeros_like(impulse))[:, ::-1]
    result = lax.conv_general_dilated(
        series[None],
        kernel_taps[:, None, :],
        window_strides=(1,),
        padding=[(impulse_len - 1, 0)],
        dimension_numbers=("NCH", "OIH", "NCH"),
        feature_group_count=series.shape[0],
        precision=lax.Precision.HIGHEST,
    )
    return result[0]


def panel_moments(pressure, halo, band, block):
    rows = pressure.shape[0]
    padded = jnp.concatenate([halo, pressure], axis=0)
    width = band.shape[1]
    parts = [
        dot(band, padded[o : o + width], ((1,), (0,))) for o in range(0, rows, block)
    ]
    filtered = jnp.concatenate(parts, axis=0).astype(BF16)
    wide = filtered.astype(F32)
    mean = jnp.mean(wide, axis=0)
    spread = jnp.sum(jnp.square(wide - mean[None, :]), axis=0)
    return mean, spread


def body(pressure, fir_taps, influence, mode_impulse, mode_taps):
    nx, ng = lax.axis_size("gx"), lax.axis_size(("gy", "gz"))
    rows, panels = pressure.shape
    total = rows * nx
    rim = fir_taps.shape[0] - 1
    modes = influence.shape[0]
    own = modes // (nx * ng)
    own_panels = panels // nx
    block = min(512, rows)

    lines = lax.all_gather(influence.reshape(modes, -1), "gx", axis=1, tiled=True)
    halo = lax.ppermute(pressure[rows - rim :], "gx", [(i, i + 1) for i in range(nx - 1)])

    raw = dot(lines, pressure, ((1,), (1,)))
    raw = lax.psum_scatter(
        raw.reshape(nx, ng * own, rows), ("gy", "gz"), scatter_dimension=1, tiled=True
    )
    raw = lax.all_to_all(raw, "gx", split_axis=0, concat_axis=0, tiled=True)
    raw = raw.transpose(1, 0, 2).reshape(own, total)

    forward = band_matrix(fir_taps, 512)
    backward = band_matrix(fir_taps[::-1], 512)
    width = forward.shape[1]
    padded = jnp.pad(raw, ((0, 0), (rim, 0)))
    high = padded.astype(BF16)
    low = (padded - high.astype(F32)).astype(BF16)
    loads = sum(
        dot(windows(x, 512, width).reshape(-1, width), backward, ((1,), (1,)))
        for x in (high, low)
    ).reshape(own, total)

    first_mode = lax.axis_index(("gx", "gy", "gz")) * own
    own_impulse = lax.dynamic_slice_in_dim(mode_impulse, first_mode, own, 0)
    own_limits = lax.dynamic_slice_in_dim(mode_taps, first_mode, own, 0)
    responses = dynamic_filter(loads, own_impulse, own_limits).astype(BF16)

    resp_wide = responses.astype(F32)
    mean_mode = jnp.mean(resp_wide, axis=1)
    spread_mode = jnp.sqrt(jnp.mean(jnp.square(resp_wide - mean_mode[:, None]), axis=1) + 1e-06)
    ahead = windows(jnp.pad(responses, ((0, 0), (0, rim))), 512, width).reshape(-1, width)
    back = dot(ahead, forward, ((1,), (1,))).reshape(own, total)
    left = total - 1 - jnp.arange(total, dtype=jnp.int32)
    within = jnp.arange(rim + 1, dtype=jnp.int32)[:, None] <= left[None, :]
    reach = jnp.sum(jnp.where(within, fir_taps.astype(F32)[:, None], 0.0), axis=0)
    scale = 1.0 / (math.sqrt(total) * spread_mode)
    back = ((back - mean_mode[:, None] * reach[None, :]) * scale[:, None]).astype(BF16)

    back = back.reshape(own, nx, rows).transpose(1, 0, 2)
    back = lax.all_to_all(back, "gx", split_axis=0, concat_axis=0, tiled=True)
    back = lax.all_gather(back, ("gy", "gz"), axis=1, tiled=True).reshape(modes, rows)

    cross = dot(back, pressure, ((1,), (0,))).astype(BF16)
    cross = lax.all_to_all(
        cross.reshape(modes, nx, own_panels), "gx", split_axis=1, concat_axis=1, tiled=True
    )
    cross = jnp.sum(cross.astype(F32), axis=1)

    mean_part, square_part = panel_moments(
        pressure, halo, band_matrix(fir_taps[::-1], block), block
    )
    moments = jnp.stack([mean_part, square_part]).reshape(2, nx, own_panels)
    moments = lax.all_to_all(moments, "gx", split_axis=1, concat_axis=1, tiled=True)
    mean_panel = jnp.mean(moments[0], axis=0)
    squares = jnp.sum(
        moments[1] + rows * jnp.square(moments[0] - mean_panel[None, :]), axis=0
    )
    spread_panel = jnp.sqrt(squares / total + 1e-06)
    scores = cross / spread_panel[None, :]
    return (responses, scores.reshape(influence.shape))


def solution(mesh):
    return jax.shard_map(
        body,
        mesh=mesh,
        in_specs=(
            P(("wind", "gx"), ("gy", "gz")),
            P(),
            P(None, ("gy", "gz"), "gx", None),
            P(),
            P(),
        ),
        out_specs=(P(("wind", "gx", "gy", "gz"), None), P("wind", ("gy", "gz"), "gx", None)),
        check_vma=False,
    )
```

time: 280 us -> 196 us (0.70)
  waiting for transfers between devices: 198 us -> 92 us
  starting transfers between devices: 6.67 us -> 22.2 us
  local copies, waits for them, and re-layouts: 29.5 us -> 20 us
  matrix products: 22.6 us -> 29.8 us
  blocking collectives: 0 us -> 6.99 us
    all_to_all x1 -> x4, waiting for transfers between devices: 91.1 us -> 35.2 us  [the longest x1 26.2 us: body(): lax.all_to_all(cross.reshape(modes, nx, own_panels), 'gx', split_axis=1,...]
    unnamed x3, waiting for transfers between devices: 70.8 us -> 30.4 us
    unnamed x24 -> x37, local copies, waits for them, and re-layouts: 18.8 us -> 2.52 us
    all_to_all x1 -> x4, starting transfers between devices: 6.45 us -> 16.2 us  [the longest x1 5.04 us: body(): lax.all_to_all(cross.reshape(modes, nx, own_panels), 'gx', split_axis=1,...]
    all_gather x1, waiting for transfers between devices: 35.9 us -> 26.4 us  [body(): lax.all_gather(influence.reshape(modes, -1), 'gx', axis=1, tiled=True)]
    all_gather x0 -> x1, blocking collectives: none -> 6.99 us  [body(): lax.all_gather(back, ('gy', 'gz'), axis=1, tiled=True).reshape(modes, rows)]
    all_to_all x1 -> x0, local copies, waits for them, and re-layouts: 6.23 us -> none  [body(): lax.all_to_all(pressure, 'gx', split_axis=1, concat_axis=0, tiled=True)]
    ppermute x0 -> x1, starting transfers between devices: none -> 5.89 us  [body(): lax.ppermute(pressure[rows - rim:], 'gx', [(i, i + 1) for i in range(nx -...]
  transfers between devices with their start and end apart: 3 -> 7, of which waited for: 3 -> 5; matrix products, arithmetic and copies ran while one was open for 2% -> 18% of each run, Pallas kernels for 0% -> 0%
where the time goes in v1:
time: 196 us
  waiting for transfers between devices  92 us (47%)
  matrix products  29.8 us (15%)
  starting transfers between devices  22.2 us (11%)
  local copies, waits for them, and re-layouts  20 us (10%)
  between operations  15.2 us (8%)
  other arithmetic  9.45 us (5%)
  blocking collectives  6.99 us (4%)
    unnamed x3, waiting for transfers between devices  30.4 us
    all_gather x1, waiting for transfers between devices, body(): lax.all_gather(influence.reshape(modes, -1), 'gx', axis=1, tiled=True)  26.4 us
    all_to_all x1, waiting for transfers between devices, body(): lax.all_to_all(cross.reshape(modes, nx, own_panels), 'gx', split_axis=1,...  26.2 us
    dot_general x7, matrix products, dot(): lax.dot_general(a, b, (contract, ((), ())), preferred_element_type=F32)  17.1 us
    conv_general_dilated x1, matrix products, dynamic_filter(): lax.conv_general_dilated(series[None], kernel_taps[:, None, :], window_st...  12.7 us
    all_gather x1, blocking collectives, body(): lax.all_gather(back, ('gy', 'gz'), axis=1, tiled=True).reshape(modes, rows)  6.99 us
    all_to_all x1, waiting for transfers between devices, body(): raw = lax.all_to_all(raw, 'gx', split_axis=0, concat_axis=0, tiled=True)  6.18 us
    ppermute x1, starting transfers between devices, body(): lax.ppermute(pressure[rows - rim:], 'gx', [(i, i + 1) for i in range(nx -...  5.89 us
  transfers between devices with their start and end apart: 7, of which 5 were waited for; matrix products, arithmetic and copies ran while one was open for 18% of the time, Pallas kernels for 0%

profile of v1, /device:TPU:0, one launch (start us, length us, event | category | flops | bytes accessed | tf_op | source)
XLA Modules:
  0.0 195.6 jit_solution(10294810391997105271)
XLA Ops:
  8.0 2.3 %slice.128 = bf16[256,2048]{1,0:T(8,128)(2,1)} slice(bf16[1024,2048]{1,0:T(8,128)(2,1)} %param.5), slice={[768:1024], [0:2048]} | slice | bytes 2097152 | tf_op jit(solution)/shard_map/slice | solution.py:69
  10.3 5.9 %collective-permute-start = (bf16[256,2048]{1,0:T(8,128)(2,1)}, bf16[256,2048]{1,0:T(8,128)(2,1)}, u32[]{:S(2)}, u32[]{:S(2)}) collective-permute-start(bf16[256,2048]{1,0:T(8,128)(2,1)} %slice.128), channel_id=1, source_target_pairs={{0,4},{4,8},{8,12},{1,5},{5,9},{9,13},{2,6},{6,10},{10,14},{3,7},{... | collective-permute-start | bytes 3145736 | tf_op jit(solution)/shard_map/ppermute | solution.py:69
  18.5 1.3 tile.9
  22.3 1.6 reshape.135
  23.8 3.7 %fusion.7 = bf16[512,2048]{1,0:T(8,128)(2,1)S(1)} fusion(bf16[512,768]{1,0:T(8,128)(2,1)S(1)} %reshape.132, bf16[1024,2048]{1,0:T(8,128)(2,1)} %param.5), kind=kOutput, calls=%fused_computation.13 | convolution fusion | flops 1611661312 | bytes 6029312 | tf_op jit(solution)/shard_map/dot_general | solution.py:13
  27.5 26.4 %all-gather.3.cloned.1.call-done = bf16[256,1,1,2048]{3,0,2,1:T(8,128)(2,1)} async-done(((bf16[256,1,1,512]{3,0,2,1:T(8,128)(2,1)}), bf16[256,1,1,2048]{3,0,2,1:T(8,128)(2,1)}) %all-gather.3.cloned.1.call-update) | async-done | bytes 1048592 | tf_op jit(solution)/shard_map/all_gather | solution.py:68
  54.0 3.8 %fusion.17 = f32[256,1024]{1,0:T(8,128)S(1)} fusion(bf16[1024,2048]{1,0:T(8,128)(2,1)} %param.5, bf16[256,1,1,2048]{3,0,2,1:T(8,128)(2,1)} %all-gather.3.cloned.1.call-done), kind=kOutput, calls=%fused_computation.26 | convolution fusion | flops 1073741824 | bytes 6291456 | tf_op jit(solution)/shard_map/dot_general | solution.py:13
  57.8 1.7 copy.44
  61.5 5.0 %fusion.6 = bf16[512,2048]{1,0:T(8,128)(2,1)} fusion(bf16[512,768]{1,0:T(8,128)(2,1)S(1)} %reshape.132, bf16[1024,2048]{1,0:T(8,128)(2,1)} %param.5, bf16[256,2048]{1,0:T(8,128)(2,1)} %collective-permute-done), kind=kOutput, calls=%fused_computation.12 | convolution fusion | flops 1617952768 | bytes 8126464 | tf_op jit(solution)/shard_map/dot_general | solution.py:13
  66.5 29.7 %all-reduce.7.cloned.1.call-done = f32[4,64,1024]{2,0,1:T(4,128)} async-done(((f32[4,64,1024]{2,0,1:T(4,128)}), f32[4,64,1024]{2,0,1:T(4,128)}) %all-reduce.7.cloned.1.call-update) | async-done | bytes 1048592
  98.0 4.6 %all-to-all-start = ((f32[4,16,1024]{2,1,0:T(8,128)}), f32[4,16,1024]{2,1,0:T(8,128)S(1)}, u32[]{:S(2)}, u32[]{:S(2)}) async-start(f32[4,16,1024]{2,1,0:T(8,128)} %copy.45), calls=%async_computation | async-start | bytes 524288 | tf_op jit(solution)/shard_map/all_to_all | solution.py:75
  102.6 2.2 %convert_reduce_fusion = f32[2048]{0:T(1024)S(1)} fusion(bf16[512,2048]{1,0:T(8,128)(2,1)S(1)} %fusion.7, bf16[512,2048]{1,0:T(8,128)(2,1)} %fusion.6), kind=kLoop, calls=%fused_computation.1 | loop fusion | flops 10483712 | bytes 4202496 | tf_op jit(solution)/shard_map/reduce_sum | solution.py:53
  104.9 6.2 %all-to-all-done = f32[4,16,1024]{2,1,0:T(8,128)S(1)} async-done(((f32[4,16,1024]{2,1,0:T(8,128)}), f32[4,16,1024]{2,1,0:T(8,128)S(1)}, u32[]{:S(2)}, u32[]{:S(2)}) %all-to-all-start) | async-done | bytes 262176 | tf_op jit(solution)/shard_map/all_to_all | solution.py:75
  112.5 2.0 %copy.50 = f32[16,1,8,520]{0,2,3,1:T(8,128)} copy(f32[16,1,8,520]{3,2,0,1:T(8,128)S(1)} %reshape.141) | data formatting | bytes 532480 | tf_op jit(solution)/shard_map/conv_general_dilated | solution.py:32
  115.5 12.7 %fusion.11 = bf16[8,520,16]{2,0,1:T(8,128)(2,1)} fusion(f32[16,1,64]{0,1,2:T(1,128)S(1)} %bitcast.169, f32[16,1,7,63]{0,2,3,1:T(8,128)S(1)} %slice.152, f32[16,1,8,520]{0,2,3,1:T(8,128)} %copy.50), kind=kOutput, calls=%fused_computation.17 | convolution fusion | flops 51341952 | bytes 431680 | tf_op jit(solution)/shard_map/conv_general_dilated | solution.py:32
  128.2 1.8 copy.52
  132.2 3.3 %all-to-all-start.1 = ((bf16[4,16,1024]{2,1,0:T(8,128)(2,1)}), bf16[4,16,1024]{2,1,0:T(8,128)(2,1)S(1)}, u32[]{:S(2)}, u32[]{:S(2)}) async-start(bf16[4,16,1024]{2,1,0:T(8,128)(2,1)} %fusion.31), calls=%async_computation.1 | async-start | bytes 262144 | tf_op jit(solution)/shard_map/all_to_all | solution.py:106
  135.5 2.4 %fusion.1 = f32[2048]{0:T(1024)S(1)} fusion(f32[2048]{0:T(1024)S(1)} %broadcast_multiply_fusion, bf16[512,2048]{1,0:T(8,128)(2,1)S(1)} %fusion.7, bf16[512,2048]{1,0:T(8,128)(2,1)} %fusion.6), kind=kLoop, calls=%fused_computation.3 | loop fusion | flops 14678016 | bytes 4210688 | tf_op jit(solution)/shard_map/reduce_sum | solution.py:54
  138.6 2.8 %all-to-all-done.1 = bf16[4,16,1024]{2,1,0:T(8,128)(2,1)S(1)} async-done(((bf16[4,16,1024]{2,1,0:T(8,128)(2,1)}), bf16[4,16,1024]{2,1,0:T(8,128)(2,1)S(1)}, u32[]{:S(2)}, u32[]{:S(2)}) %all-to-all-start.1) | async-done | bytes 131104 | tf_op jit(solution)/shard_map/all_to_all | solution.py:106
  141.4 3.2 %all-to-all-start.3 = ((f32[2,4,512]{2,0,1:T(2,128)}), f32[2,4,512]{2,0,1:T(2,128)S(1)}, u32[]{:S(2)}, u32[]{:S(2)}) async-start(f32[2,4,512]{2,0,1:T(2,128)} %pad_maximum_fusion.5), calls=%async_computation.3 | async-start | bytes 32768 | tf_op jit(solution)/shard_map/all_to_all | solution.py:119
  144.7 7.0 %all_gather.7 = bf16[4,64,1024]{2,1,0:T(8,128)(2,1)S(1)} all-gather(bf16[4,16,1024]{2,1,0:T(8,128)(2,1)S(1)} %all-to-all-done.1), channel_id=1, replica_groups=mesh['wind'=2,'gx'=4,'gy'=2,'gz'=2] {'gy','gz'}, dimensions={1}, use_global_device_ids=true | all-gather | bytes 655360 | tf_op jit(solution)/shard_map/all_gather | solution.py:107
  151.7 3.5 %convolution_convert_fusion = bf16[256,2048]{1,0:T(8,128)(2,1)S(1)} fusion(bf16[256,1024]{1,0:T(8,128)(2,1)S(1)} %bitcast.166, bf16[1024,2048]{1,0:T(8,128)(2,1)} %param.5), kind=kOutput, calls=%fused_computation.14 | convolution fusion | flops 1074266112 | bytes 5767168 | tf_op jit(solution)/shard_map/dot_general | solution.py:13
  156.2 5.0 %all-to-all-start.2 = ((bf16[256,4,512]{2,0,1:T(8,128)(2,1)}), bf16[256,4,512]{2,0,1:T(8,128)(2,1)S(1)}, u32[]{:S(2)}, u32[]{:S(2)}) async-start(bf16[256,4,512]{2,0,1:T(8,128)(2,1)} %bitcast.160), calls=%async_computation.2 | async-start | bytes 2097152 | tf_op jit(solution)/shard_map/all_to_all | solution.py:110
  161.3 26.2 %all-to-all-done.2 = bf16[256,4,512]{2,0,1:T(8,128)(2,1)S(1)} async-done(((bf16[256,4,512]{2,0,1:T(8,128)(2,1)}), bf16[256,4,512]{2,0,1:T(8,128)(2,1)S(1)}, u32[]{:S(2)}, u32[]{:S(2)}) %all-to-all-start.2) | async-done | bytes 1048608 | tf_op jit(solution)/shard_map/all_to_all | solution.py:110
  (90 shorter events, 16.0 us)
Async XLA Ops:
  7.2 13.4 %copy-start.4 = (s32[256]{0:T(256)S(1)}, s32[256]{0:T(256)}, u32[]{:S(2)}) copy-start(s32[256]{0:T(256)} %param.9) | copy-start | bytes 3076
  7.2 13.5 %copy-start.2 = (f32[256,64]{0,1:T(8,128)S(1)}, f32[256,64]{0,1:T(8,128)}, u32[]{:S(2)}) copy-start(f32[256,64]{0,1:T(8,128)} %param.8) | copy-start | bytes 196612
  7.2 46.8 %all-gather.3.cloned.1.call-start = ((), (), s32[]{:S(2)}) async-start(), calls=%async_computation.4 | async-start | bytes 1310720 | tf_op jit(solution)/shard_map/all_gather | solution.py:68
  7.9 88.3 %all-reduce.7.cloned.1.call-start = ((), (), s32[]{:S(2)}) async-start(), calls=%async_computation.5 | async-start | bytes 2097152
  10.3 51.2 %collective-permute-start = (bf16[256,2048]{1,0:T(8,128)(2,1)}, bf16[256,2048]{1,0:T(8,128)(2,1)}, u32[]{:S(2)}, u32[]{:S(2)}) collective-permute-start(bf16[256,2048]{1,0:T(8,128)(2,1)} %slice.128), channel_id=1, source_target_pairs={{0,4},{4,8},{8,12},{1,5},{5,9},{9,13},{2,6},{6,10},{10,14},{3,7},{... | collective-permute-start | bytes 3145736 | tf_op jit(solution)/shard_map/ppermute | solution.py:69
  27.5 32.7 %copy-start.5 = (u32[32]{0:T(128)S(1)}, u32[32]{0:T(128)}, u32[]{:S(2)}) copy-start(u32[32]{0:T(128)} %constant.69) | copy-start | bytes 388
  98.0 13.0 %all-to-all-start = ((f32[4,16,1024]{2,1,0:T(8,128)}), f32[4,16,1024]{2,1,0:T(8,128)S(1)}, u32[]{:S(2)}, u32[]{:S(2)}) async-start(f32[4,16,1024]{2,1,0:T(8,128)} %copy.45), calls=%async_computation | async-start | bytes 524288 | tf_op jit(solution)/shard_map/all_to_all | solution.py:75
  115.5 14.6 %copy-start.3 = (pred[8,520]{1,0:T(8,128)(4,1)S(1)}, pred[8,520]{1,0:T(8,128)(4,1)}, u32[]{:S(2)}) copy-start(pred[8,520]{1,0:T(8,128)(4,1)} %constant.66) | copy-start | bytes 12484
  115.5 15.3 %copy-start = (bf16[512,768]{1,0:T(8,128)(2,1)S(1)}, bf16[512,768]{1,0:T(8,128)(2,1)}, u32[]{:S(2)}) copy-start(bf16[512,768]{1,0:T(8,128)(2,1)} %reshape.135) | copy-start | bytes 2359300
  130.5 24.6 %copy-start.1 = (bf16[16,4096]{1,0:T(8,128)(2,1)}, bf16[16,4096]{1,0:T(8,128)(2,1)S(1)}, u32[]{:S(2)}) copy-start(bf16[16,4096]{1,0:T(8,128)(2,1)S(1)} %get-tuple-element.3) | copy-start | bytes 393220
  132.2 9.2 %all-to-all-start.1 = ((bf16[4,16,1024]{2,1,0:T(8,128)(2,1)}), bf16[4,16,1024]{2,1,0:T(8,128)(2,1)S(1)}, u32[]{:S(2)}, u32[]{:S(2)}) async-start(bf16[4,16,1024]{2,1,0:T(8,128)(2,1)} %fusion.31), calls=%async_computation.1 | async-start | bytes 262144 | tf_op jit(solution)/shard_map/all_to_all | solution.py:106
  141.4 14.8 %all-to-all-start.3 = ((f32[2,4,512]{2,0,1:T(2,128)}), f32[2,4,512]{2,0,1:T(2,128)S(1)}, u32[]{:S(2)}, u32[]{:S(2)}) async-start(f32[2,4,512]{2,0,1:T(2,128)} %pad_maximum_fusion.5), calls=%async_computation.3 | async-start | bytes 32768 | tf_op jit(solution)/shard_map/all_to_all | solution.py:119
  156.2 31.3 %all-to-all-start.2 = ((bf16[256,4,512]{2,0,1:T(8,128)(2,1)}), bf16[256,4,512]{2,0,1:T(8,128)(2,1)S(1)}, u32[]{:S(2)}, u32[]{:S(2)}) async-start(bf16[256,4,512]{2,0,1:T(8,128)(2,1)} %bitcast.160), calls=%async_computation.2 | async-start | bytes 2097152 | tf_op jit(solution)/shard_map/all_to_all | solution.py:110
Sparse Core Ops, SparseCore 0:
  9.6 44.3 all-gather.2
  59.6 36.5 all-reduce.6

commit v2 on v1

--- a/solution.py
+++ b/solution.py
@@ -1,8 +1,11 @@
+import functools
 import math
 
 import jax
 import jax.numpy as jnp
 from jax import lax
+from jax.experimental import pallas as pl
+from jax.experimental.pallas import tpu as pltpu
 from jax.sharding import PartitionSpec as P
 
 F32 = jnp.float32
@@ -55,7 +58,7 @@
     return mean, spread
 
 
-def body(pressure, fir_taps, influence, mode_impulse, mode_taps):
+def plain_body(pressure, fir_taps, influence, mode_impulse, mode_taps):
     nx, ng = lax.axis_size("gx"), lax.axis_size(("gy", "gz"))
     rows, panels = pressure.shape
     total = rows * nx
@@ -124,6 +127,327 @@
     spread_panel = jnp.sqrt(squares / total + 1e-06)
     scores = cross / spread_panel[None, :]
     return (responses, scores.reshape(influence.shape))
+
+
+SPAN = 512
+LEAD = 128
+COLS = 256
+
+
+def tower_kernel(
+    nx, own, dyn, infl, press, taps, gains, resp, score,
+    lines, raw, from_core, core_sum, from_pair, pair_sum, slots, series, loads, wide_gain,
+    modal, band_back, band_fwd, halo, filt, turned, back, part, arrived, moments, moved,
+    send, recv,
+):
+    rows, panels = press.shape
+    modes, own_panels = infl.shape
+    total = rows * nx
+    rim = halo.shape[0]
+    spans = total // SPAN
+    gx, gy, gz = lax.axis_index("gx"), lax.axis_index("gy"), lax.axis_index("gz")
+    mesh_id = pl.DeviceIdType.MESH
+
+    def remote(src, dst, sem, device):
+        return pltpu.make_async_remote_copy(
+            src_ref=src, dst_ref=dst, send_sem=send.at[sem], recv_sem=recv.at[sem],
+            device_id=device, device_id_type=mesh_id,
+        )
+
+    def ahead(d):
+        return lax.rem(gx + d, nx)
+
+    def behind(d):
+        return lax.rem(gx + nx - d, nx)
+
+    def columns(index, size):
+        return pl.ds(pl.multiple_of(index * size, size), size)
+
+    hops = range(1, nx)
+    first = {name: i * nx for i, name in enumerate(("lines", "raw", "back", "cross", "moments"))}
+    extra = 5 * nx
+
+    barrier = pltpu.get_barrier_semaphore()
+    peers = [{"gx": ahead(d)} for d in hops] + [{"gy": 1 - gy}, {"gz": 1 - gz}]
+    for peer in peers:
+        pl.semaphore_signal(barrier, inc=1, device_id=peer, device_id_type=mesh_id)
+    pl.semaphore_wait(barrier, len(peers))
+
+    line_copies = [
+        remote(infl, lines.at[d], first["lines"] + d, {"gx": ahead(d)}) for d in hops
+    ]
+    for copy in line_copies:
+        copy.start()
+    halo_copy = remote(press.at[pl.ds(rows - rim, rim)], halo, extra, {"gx": ahead(1)})
+
+    width = band_back.shape[1]
+    for c in range(SPAN // LEAD):
+        for k, band in ((0, band_fwd), (1, band_back)):
+            line = jnp.broadcast_to(taps[pl.ds(k, 1), :], (LEAD, width))
+            band[pl.ds(c * LEAD, LEAD), :] = pltpu.roll(
+                line, c * LEAD, 1, stride=1, stride_axis=0
+            ).astype(BF16)
+    for k in range(dyn):
+        wide_gain[k] = jnp.broadcast_to(gains[:, k : k + 1], (own, LEAD))
+    series[:, pl.ds(0, rim)] = jnp.zeros((own, rim), F32)
+    loads[:, pl.ds(0, LEAD)] = jnp.zeros((own, LEAD), F32)
+    modal[:, pl.ds(total, rim)] = jnp.zeros((own, rim), BF16)
+    moments[...] = jnp.zeros(moments.shape, F32)
+
+    @pl.when(gx == 0)
+    def _():
+        halo[...] = jnp.zeros(halo.shape, BF16)
+
+    def add_lines(block, held, fresh):
+        def step(i, _):
+            at = columns(i, COLS)
+            piece = press[at, columns(block, own_panels)]
+            term = dot(held[...], piece, ((1,), (1,))).reshape(nx, 2, 2, own, COLS)
+            if fresh:
+                raw[:, :, :, :, at] = term
+            else:
+                raw[:, :, :, :, at] += term
+            return 0
+
+        lax.fori_loop(0, rows // COLS, step, 0)
+
+    add_lines(gx, infl, True)
+
+    def filter_later(i, _):
+        at = columns(i, COLS)
+        for o in range(SPAN, rows, SPAN):
+            piece = press[pl.ds(o - rim, SPAN + rim), at]
+            filt[pl.ds(o, SPAN), at] = dot(band_back[...], piece, ((1,), (0,))).astype(BF16)
+        return 0
+
+    lax.fori_loop(0, panels // COLS, filter_later, 0)
+
+    for d, copy in zip(hops, line_copies):
+        copy.wait_recv()
+        add_lines(behind(d), lines.at[d], False)
+
+    core_copy = remote(raw.at[:, :, 1 - gz], from_core, extra + 1, {"gz": 1 - gz})
+    core_copy.start()
+    core_copy.wait_recv()
+    core_sum[...] = raw[:, :, gz] + from_core[...]
+    pair_copy = remote(core_sum.at[:, 1 - gy], from_pair, extra + 2, {"gy": 1 - gy})
+    pair_copy.start()
+    pair_copy.wait_recv()
+    pair_sum[...] = core_sum[:, gy] + from_pair[...]
+    raw_copies = [
+        remote(pair_sum.at[ahead(d)], slots.at[d], first["raw"] + d, {"gx": ahead(d)})
+        for d in hops
+    ]
+    for copy in raw_copies:
+        copy.start()
+
+    @pl.when(gx < nx - 1)
+    def _():
+        halo_copy.start()
+
+    def place(block):
+        return pl.ds(pl.multiple_of(block * rows + rim, LEAD), rows)
+
+    series[:, place(gx)] = pair_sum[gx]
+    for d, copy in zip(hops, raw_copies):
+        copy.wait_recv()
+        series[:, place(behind(d))] = slots[d]
+
+    high, low = [], []
+    for i in range(spans):
+        piece = series[:, pl.ds(i * SPAN, SPAN + rim)]
+        top = piece.astype(BF16)
+        high.append(top)
+        low.append((piece - top.astype(F32)).astype(BF16))
+    both = dot(jnp.concatenate(high + low, axis=0), band_back[...], ((1,), (1,)))
+    for i in range(spans):
+        loads[:, pl.ds(LEAD + i * SPAN, SPAN)] = (
+            both[i * own : (i + 1) * own] + both[(spans + i) * own : (spans + i + 1) * own]
+        )
+
+    def respond(i, _):
+        piece = loads[:, pl.ds(pl.multiple_of(i * SPAN, SPAN), SPAN + LEAD)]
+        result = jnp.zeros((own, SPAN), F32)
+        for k in range(dyn):
+            gain = jnp.concatenate([wide_gain[k]] * (SPAN // LEAD), axis=1)
+            moved_by = piece if k == 0 else pltpu.roll(piece, k, 1)
+            result = result + gain * moved_by[:, LEAD:]
+        modal[:, columns(i, SPAN)] = result.astype(BF16)
+        return 0
+
+    lax.fori_loop(0, spans, respond, 0)
+
+    settled = modal[:, pl.ds(0, total)]
+    resp[...] = settled
+    wide = settled.astype(F32)
+    mean_mode = jnp.mean(wide, axis=1, keepdims=True)
+    off = wide - mean_mode
+    spread_mode = jnp.sqrt(jnp.mean(off * off, axis=1, keepdims=True) + 1e-06)
+    scale = 1.0 / (math.sqrt(total) * spread_mode)
+
+    later = [modal[:, pl.ds(i * SPAN, SPAN + rim)] for i in range(spans)]
+    lane = lax.broadcasted_iota(jnp.int32, (own, width), 1)
+    full = jnp.ones((own, width), F32).astype(BF16)
+    cut = jnp.where(lane < SPAN, 1.0, 0.0).astype(BF16)
+    turned_wide = dot(jnp.concatenate(later + [full, cut], axis=0), band_fwd[...], ((1,), (1,)))
+    reach = [turned_wide[(spans + j) * own : (spans + j + 1) * own] for j in range(2)]
+    for i in range(spans):
+        value = turned_wide[i * own : (i + 1) * own] - mean_mode * reach[int(i == spans - 1)]
+        block, offset = divmod(i * SPAN, rows)
+        turned[block, :, pl.ds(offset, SPAN)] = (value * scale).astype(BF16)
+
+    back_copies = [
+        remote(turned.at[ahead(d)], back.at[gx, gy, gz], first["back"] + d, {"gx": ahead(d)})
+        for d in hops
+    ]
+    for copy in back_copies:
+        copy.start()
+    back[gx, gy, gz] = turned[gx]
+
+    @pl.when(gx > 0)
+    def _():
+        halo_copy.wait_recv()
+
+    def filter_first(i, _):
+        at = columns(i, COLS)
+        value = dot(band_back[:, pl.ds(0, rim)], halo[:, at], ((1,), (0,)))
+        value += dot(band_back[:, pl.ds(rim, SPAN)], press[pl.ds(0, SPAN), at], ((1,), (0,)))
+        filt[pl.ds(0, SPAN), at] = value.astype(BF16)
+        return 0
+
+    def measure(block, slot):
+        for j in range(own_panels // COLS):
+            at = pl.ds(pl.multiple_of(block * own_panels + j * COLS, COLS), COLS)
+            values = filt[:, at].astype(F32)
+            mean = jnp.mean(values, axis=0, keepdims=True)
+            gap = values - mean
+            moments[slot, pl.ds(0, 1), pl.ds(j * COLS, COLS)] = mean
+            moments[slot, pl.ds(1, 1), pl.ds(j * COLS, COLS)] = jnp.sum(
+                gap * gap, axis=0, keepdims=True
+            )
+
+    lax.fori_loop(0, panels // COLS, filter_first, 0)
+    moment_copies = []
+    for d in range(nx):
+        measure(ahead(d), d)
+        if d:
+            copy = remote(moments.at[d], moved.at[d], first["moments"] + d, {"gx": ahead(d)})
+            copy.start()
+            moment_copies.append(copy)
+
+    for copy in back_copies:
+        copy.wait_recv()
+    mine = back.at[:, gy, gz]
+    back_pair = remote(mine, mine, extra + 3, {"gy": 1 - gy})
+    back_core = remote(mine, mine, extra + 4, {"gz": 1 - gz})
+    back_pair.start()
+    back_core.start()
+    back_pair.wait_recv()
+    other = back.at[:, 1 - gy, gz]
+    back_forward = remote(other, other, extra + 5, {"gz": 1 - gz})
+    back_forward.start()
+    back_core.wait_recv()
+    back_forward.wait_recv()
+
+    def cross_block(block, j):
+        at = pl.ds(pl.multiple_of(block * own_panels + j * COLS, COLS), COLS)
+        return dot(back[...].reshape(modes, rows), press[:, at], ((1,), (0,)))
+
+    cross_copies = []
+    for d in hops:
+        for j in range(own_panels // COLS):
+            part[d, :, pl.ds(j * COLS, COLS)] = cross_block(ahead(d), j).astype(BF16)
+        copy = remote(part.at[d], arrived.at[d], first["cross"] + d, {"gx": ahead(d)})
+        copy.start()
+        cross_copies.append(copy)
+    for j in range(own_panels // COLS):
+        score[:, pl.ds(j * COLS, COLS)] = cross_block(gx, j)
+
+    for copy in moment_copies:
+        copy.wait_recv()
+    means = [moments[0, pl.ds(0, 1), :]] + [moved[d, pl.ds(0, 1), :] for d in hops]
+    squares = [moments[0, pl.ds(1, 1), :]] + [moved[d, pl.ds(1, 1), :] for d in hops]
+    mean_panel = sum(means) / nx
+    spread = sum(squares) + rows * sum(jnp.square(m - mean_panel) for m in means)
+    factor = 1.0 / jnp.sqrt(spread / total + 1e-06)
+    for copy in cross_copies:
+        copy.wait_recv()
+    value = score[...]
+    for d in hops:
+        value = value + arrived[d].astype(F32)
+    score[...] = value * factor
+
+    for copy in line_copies + raw_copies + back_copies + moment_copies + cross_copies:
+        copy.wait_send()
+    for copy in (core_copy, pair_copy, back_pair, back_core, back_forward):
+        copy.wait_send()
+
+    @pl.when(gx < nx - 1)
+    def _():
+        halo_copy.wait_send()
+
+
+def body(pressure, fir_taps, influence, mode_impulse, mode_taps):
+    nx, ny, nz = (lax.axis_size(name) for name in ("gx", "gy", "gz"))
+    rows, panels = pressure.shape
+    total = rows * nx
+    rim = fir_taps.shape[0] - 1
+    modes = influence.shape[0]
+    own = modes // (nx * ny * nz)
+    own_panels = panels // nx
+    dyn = mode_impulse.shape[1]
+    fits = own % 16 == 0 and ny == nz == 2 and rows % SPAN == 0 and own_panels % COLS == 0
+    if not fits or rim % LEAD or dyn > LEAD:
+        return plain_body(pressure, fir_taps, influence, mode_impulse, mode_taps)
+
+    first_mode = lax.axis_index(("gx", "gy", "gz")) * own
+    own_impulse = lax.dynamic_slice_in_dim(mode_impulse, first_mode, own, 0)
+    own_limits = lax.dynamic_slice_in_dim(mode_taps, first_mode, own, 0)
+    kept = jnp.arange(dyn, dtype=jnp.int32)[None, :] < own_limits[:, None]
+    gains = jnp.where(kept, own_impulse, 0.0)
+    width = SPAN + rim
+    tap_rows = jnp.stack([fir_taps, fir_taps[::-1]]).astype(F32)
+    tap_rows = jnp.pad(tap_rows, ((0, 0), (0, width - rim - 1)))
+
+    vmem = pl.BlockSpec(memory_space=pltpu.VMEM)
+    responses, scores = pl.pallas_call(
+        functools.partial(tower_kernel, nx, own, dyn),
+        out_shape=(
+            jax.ShapeDtypeStruct((own, total), BF16),
+            jax.ShapeDtypeStruct((modes, own_panels), F32),
+        ),
+        in_specs=[vmem] * 4,
+        out_specs=(vmem, vmem),
+        scratch_shapes=[
+            pltpu.VMEM((nx, modes, own_panels), BF16),
+            pltpu.VMEM((nx, 2, 2, own, rows), F32),
+            pltpu.VMEM((nx, 2, own, rows), F32),
+            pltpu.VMEM((nx, 2, own, rows), F32),
+            pltpu.VMEM((nx, own, rows), F32),
+            pltpu.VMEM((nx, own, rows), F32),
+            pltpu.VMEM((nx, own, rows), F32),
+            pltpu.VMEM((own, rim + total), F32),
+            pltpu.VMEM((own, LEAD + total), F32),
+            pltpu.VMEM((dyn, own, LEAD), F32),
+            pltpu.VMEM((own, total + rim), BF16),
+            pltpu.VMEM((SPAN, width), BF16),
+            pltpu.VMEM((SPAN, width), BF16),
+            pltpu.VMEM((rim, panels), BF16),
+            pltpu.VMEM((rows, panels), BF16),
+            pltpu.VMEM((nx, own, rows), BF16),
+            pltpu.VMEM((nx, 2, 2, own, rows), BF16),
+            pltpu.VMEM((nx, modes, own_panels), BF16),
+            pltpu.VMEM((nx, modes, own_panels), BF16),
+            pltpu.VMEM((nx, 8, own_panels), F32),
+            pltpu.VMEM((nx, 8, own_panels), F32),
+            pltpu.SemaphoreType.DMA((5 * nx + 6,)),
+            pltpu.SemaphoreType.DMA((5 * nx + 6,)),
+        ],
+        compiler_params=pltpu.CompilerParams(
+            collective_id=0, has_side_effects=True, vmem_limit_bytes=48 * 1024 * 1024
+        ),
+    )(influence.reshape(modes, own_panels), pressure, tap_rows, gains)
+    return responses, scores.reshape(influence.shape)
 
 
 def solution(mesh):

time: 196 us -> 108 us (0.55)
  the two profiles are of different devices: /device:TPU:0 before, /device:TPU:9 now
where the time goes in v2:
time: 108 us
  Pallas kernels  99.6 us (92%)
  local copies, waits for them, and re-layouts  7.62 us (7%)
    pallas_call x1, Pallas kernels, body(): pl.pallas_call(functools.partial(tower_kernel, nx, own, dyn), out_shape=(...  99.6 us
    unnamed x11, local copies, waits for them, and re-layouts  6.06 us

profile of v2, /device:TPU:9, one launch (start us, length us, event | category | flops | bytes accessed | tf_op | source)
XLA Modules:
  0.0 108.0 jit_solution(17911855097472389445)
XLA Ops:
  0.6 0.0 copy-start
  0.7 0.8 dynamic_slice.6
  1.4 0.8 reverse
  2.2 0.1 slice
  2.3 0.7 stack.9
  3.0 0.0 copy-done
  3.0 0.1 constant_dynamic-slice_fusion
  3.1 0.1 copy.9
  3.1 0.1 fusion.gains
  3.2 0.0 copy-start.1
  3.2 2.2 %copy-done.1 = bf16[1024,2048]{1,0:T(8,128)(2,1)S(1)} copy-done((bf16[1024,2048]{1,0:T(8,128)(2,1)S(1)}, bf16[1024,2048]{1,0:T(8,128)(2,1)}, u32[]{:S(2)}) %copy-start.1) | copy-done | bytes 4194328
  5.4 0.0 copy-start.2
  5.4 0.9 copy-done.2
  6.4 99.6 %shard_map.68 = (bf16[16,4096]{1,0:T(8,128)(2,1)S(1)}, f32[256,512]{1,0:T(8,128)S(1)}) custom-call(bf16[256,512]{1,0:T(8,128)(2,1)S(1)} %bitcast.4, bf16[1024,2048]{1,0:T(8,128)(2,1)S(1)} %copy-done.1, f32[2,768]{1,0:T(2,128)S(1)} %fusion.4.taps, f32[16,64]{1,0:T(8,128)S(1)} %fusion.gains), custom_call_target="tpu_custom_call" | custom-call | tf_op jit(solution)/shard_map/pallas_call | solution.py:413
  106.0 1.3 %copy.8 = f32[256,1,1,512]{3,2,1,0:T(1,128)} copy(f32[256,1,1,512]{3,0,2,1:T(8,128)S(1)} %bitcast.3) | data formatting | bytes 1048576
  107.3 0.7 copy.11
  (2 shorter events, 0.0 us)
Async XLA Ops:
  0.6 2.4 %copy-start = (f32[256,64]{0,1:T(8,128)S(1)}, f32[256,64]{0,1:T(8,128)}, u32[]{:S(2)}) copy-start(f32[256,64]{0,1:T(8,128)} %param.8) | copy-start | bytes 196612
  3.2 2.2 %copy-start.1 = (bf16[1024,2048]{1,0:T(8,128)(2,1)S(1)}, bf16[1024,2048]{1,0:T(8,128)(2,1)}, u32[]{:S(2)}) copy-start(bf16[1024,2048]{1,0:T(8,128)(2,1)} %press.1) | copy-start | bytes 12582916
  5.4 0.9 copy-start.2

commit v3 on v2

--- a/solution.py
+++ b/solution.py
@@ -135,7 +135,7 @@
 
 
 def tower_kernel(
-    nx, own, dyn, infl, press, taps, gains, resp, score,
+    nx, own, dyn, infl, outside, taps, gains, resp, score, press, fetched,
     lines, raw, from_core, core_sum, from_pair, pair_sum, slots, series, loads, wide_gain,
     modal, band_back, band_fwd, halo, filt, turned, back, part, arrived, moments, moved,
     send, recv,
@@ -145,6 +145,7 @@
     total = rows * nx
     rim = halo.shape[0]
     spans = total // SPAN
+    wind = lax.axis_index("wind")
     gx, gy, gz = lax.axis_index("gx"), lax.axis_index("gy"), lax.axis_index("gz")
     mesh_id = pl.DeviceIdType.MESH
 
@@ -164,26 +165,41 @@
         return pl.ds(pl.multiple_of(index * size, size), size)
 
     hops = range(1, nx)
-    first = {name: i * nx for i, name in enumerate(("lines", "raw", "back", "cross", "moments"))}
-    extra = 5 * nx
-
+    first = {name: i * nx for i, name in enumerate(("lines", "raw", "back", "cross", "moments", "twin"))}
+    extra = 6 * nx
+
+    fetch = pltpu.make_async_copy(outside, press, fetched)
+    fetch.start()
     barrier = pltpu.get_barrier_semaphore()
-    peers = [{"gx": ahead(d)} for d in hops] + [{"gy": 1 - gy}, {"gz": 1 - gz}]
+    peers = [{"gx": ahead(d)} for d in hops] + [{"gy": 1 - gy}, {"gz": 1 - gz}, {"wind": 1 - wind}]
     for peer in peers:
         pl.semaphore_signal(barrier, inc=1, device_id=peer, device_id_type=mesh_id)
     pl.semaphore_wait(barrier, len(peers))
 
+    share = columns(wind, modes // 2)
     line_copies = [
-        remote(infl, lines.at[d], first["lines"] + d, {"gx": ahead(d)}) for d in hops
+        remote(infl.at[share], lines.at[d, share], first["lines"] + d, {"gx": ahead(d)})
+        for d in hops
+    ]
+    twin_copies = [
+        remote(lines.at[d, share], lines.at[d, share], first["twin"] + d, {"wind": 1 - wind})
+        for d in hops
     ]
     for copy in line_copies:
         copy.start()
     halo_copy = remote(press.at[pl.ds(rows - rim, rim)], halo, extra, {"gx": ahead(1)})
 
     width = band_back.shape[1]
+    reach_to = rim + LEAD
+    cross_sum = lax.broadcasted_iota(jnp.int32, (reach_to, reach_to), 0)
+    cross_sum += lax.broadcasted_iota(jnp.int32, (reach_to, reach_to), 1)
+    flip = jnp.where(cross_sum == rim, 1.0, 0.0).astype(BF16)
+    reverse = dot(taps[:, pl.ds(0, reach_to)], flip, ((1,), (0,)))[0:1]
+    reverse = jnp.concatenate([reverse, jnp.zeros((1, width - reach_to), F32)], axis=1)
+    tap_line = taps[...].astype(F32)[0:1]
     for c in range(SPAN // LEAD):
-        for k, band in ((0, band_fwd), (1, band_back)):
-            line = jnp.broadcast_to(taps[pl.ds(k, 1), :], (LEAD, width))
+        for tap_row, band in ((tap_line, band_fwd), (reverse, band_back)):
+            line = jnp.broadcast_to(tap_row, (LEAD, width))
             band[pl.ds(c * LEAD, LEAD), :] = pltpu.roll(
                 line, c * LEAD, 1, stride=1, stride_axis=0
             ).astype(BF16)
@@ -211,6 +227,7 @@
 
         lax.fori_loop(0, rows // COLS, step, 0)
 
+    fetch.wait()
     add_lines(gx, infl, True)
 
     def filter_later(i, _):
@@ -222,9 +239,17 @@
 
     lax.fori_loop(0, panels // COLS, filter_later, 0)
 
-    for d, copy in zip(hops, line_copies):
-        copy.wait_recv()
+    order = sorted(hops, key=lambda d: min(d, nx - d))
+    for d in order:
+        line_copies[d - 1].wait_recv()
+        twin_copies[d - 1].start()
+    for d in order:
+        twin_copies[d - 1].wait_recv()
         add_lines(behind(d), lines.at[d], False)
+
+    @pl.when(gx < nx - 1)
+    def _():
+        halo_copy.start()
 
     core_copy = remote(raw.at[:, :, 1 - gz], from_core, extra + 1, {"gz": 1 - gz})
     core_copy.start()
@@ -241,10 +266,6 @@
     for copy in raw_copies:
         copy.start()
 
-    @pl.when(gx < nx - 1)
-    def _():
-        halo_copy.start()
-
     def place(block):
         return pl.ds(pl.multiple_of(block * rows + rim, LEAD), rows)
 
@@ -303,37 +324,6 @@
     for copy in back_copies:
         copy.start()
     back[gx, gy, gz] = turned[gx]
-
-    @pl.when(gx > 0)
-    def _():
-        halo_copy.wait_recv()
-
-    def filter_first(i, _):
-        at = columns(i, COLS)
-        value = dot(band_back[:, pl.ds(0, rim)], halo[:, at], ((1,), (0,)))
-        value += dot(band_back[:, pl.ds(rim, SPAN)], press[pl.ds(0, SPAN), at], ((1,), (0,)))
-        filt[pl.ds(0, SPAN), at] = value.astype(BF16)
-        return 0
-
-    def measure(block, slot):
-        for j in range(own_panels // COLS):
-            at = pl.ds(pl.multiple_of(block * own_panels + j * COLS, COLS), COLS)
-            values = filt[:, at].astype(F32)
-            mean = jnp.mean(values, axis=0, keepdims=True)
-            gap = values - mean
-            moments[slot, pl.ds(0, 1), pl.ds(j * COLS, COLS)] = mean
-            moments[slot, pl.ds(1, 1), pl.ds(j * COLS, COLS)] = jnp.sum(
-                gap * gap, axis=0, keepdims=True
-            )
-
-    lax.fori_loop(0, panels // COLS, filter_first, 0)
-    moment_copies = []
-    for d in range(nx):
-        measure(ahead(d), d)
-        if d:
-            copy = remote(moments.at[d], moved.at[d], first["moments"] + d, {"gx": ahead(d)})
-            copy.start()
-            moment_copies.append(copy)
 
     for copy in back_copies:
         copy.wait_recv()
@@ -363,6 +353,37 @@
     for j in range(own_panels // COLS):
         score[:, pl.ds(j * COLS, COLS)] = cross_block(gx, j)
 
+    @pl.when(gx > 0)
+    def _():
+        halo_copy.wait_recv()
+
+    def filter_first(i, _):
+        at = columns(i, COLS)
+        value = dot(band_back[:, pl.ds(0, rim)], halo[:, at], ((1,), (0,)))
+        value += dot(band_back[:, pl.ds(rim, SPAN)], press[pl.ds(0, SPAN), at], ((1,), (0,)))
+        filt[pl.ds(0, SPAN), at] = value.astype(BF16)
+        return 0
+
+    def measure(block, slot):
+        for j in range(own_panels // COLS):
+            at = pl.ds(pl.multiple_of(block * own_panels + j * COLS, COLS), COLS)
+            values = filt[:, at].astype(F32)
+            mean = jnp.mean(values, axis=0, keepdims=True)
+            gap = values - mean
+            moments[slot, pl.ds(0, 1), pl.ds(j * COLS, COLS)] = mean
+            moments[slot, pl.ds(1, 1), pl.ds(j * COLS, COLS)] = jnp.sum(
+                gap * gap, axis=0, keepdims=True
+            )
+
+    lax.fori_loop(0, panels // COLS, filter_first, 0)
+    moment_copies = []
+    for d in range(nx):
+        measure(ahead(d), d)
+        if d:
+            copy = remote(moments.at[d], moved.at[d], first["moments"] + d, {"gx": ahead(d)})
+            copy.start()
+            moment_copies.append(copy)
+
     for copy in moment_copies:
         copy.wait_recv()
     means = [moments[0, pl.ds(0, 1), :]] + [moved[d, pl.ds(0, 1), :] for d in hops]
@@ -377,7 +398,7 @@
         value = value + arrived[d].astype(F32)
     score[...] = value * factor
 
-    for copy in line_copies + raw_copies + back_copies + moment_copies + cross_copies:
+    for copy in line_copies + twin_copies + raw_copies + back_copies + moment_copies + cross_copies:
         copy.wait_send()
     for copy in (core_copy, pair_copy, back_pair, back_core, back_forward):
         copy.wait_send()
@@ -396,7 +417,7 @@
     own = modes // (nx * ny * nz)
     own_panels = panels // nx
     dyn = mode_impulse.shape[1]
-    fits = own % 16 == 0 and ny == nz == 2 and rows % SPAN == 0 and own_panels % COLS == 0
+    fits = own % 16 == 0 and lax.axis_size("wind") == 2 and modes % 32 == 0 and ny == nz == 2 and rows % SPAN == 0 and own_panels % COLS == 0
     if not fits or rim % LEAD or dyn > LEAD:
         return plain_body(pressure, fir_taps, influence, mode_impulse, mode_taps)
 
@@ -406,8 +427,7 @@
     kept = jnp.arange(dyn, dtype=jnp.int32)[None, :] < own_limits[:, None]
     gains = jnp.where(kept, own_impulse, 0.0)
     width = SPAN + rim
-    tap_rows = jnp.stack([fir_taps, fir_taps[::-1]]).astype(F32)
-    tap_rows = jnp.pad(tap_rows, ((0, 0), (0, width - rim - 1)))
+    tap_rows = jnp.broadcast_to(jnp.pad(fir_taps, (0, width - rim - 1))[None], (16, width))
 
     vmem = pl.BlockSpec(memory_space=pltpu.VMEM)
     responses, scores = pl.pallas_call(
@@ -416,9 +436,11 @@
             jax.ShapeDtypeStruct((own, total), BF16),
             jax.ShapeDtypeStruct((modes, own_panels), F32),
         ),
-        in_specs=[vmem] * 4,
+        in_specs=[vmem, pl.BlockSpec(memory_space=pl.ANY), vmem, vmem],
         out_specs=(vmem, vmem),
         scratch_shapes=[
+            pltpu.VMEM((rows, panels), BF16),
+            pltpu.SemaphoreType.DMA,
             pltpu.VMEM((nx, modes, own_panels), BF16),
             pltpu.VMEM((nx, 2, 2, own, rows), F32),
             pltpu.VMEM((nx, 2, own, rows), F32),
@@ -440,8 +462,8 @@
             pltpu.VMEM((nx, modes, own_panels), BF16),
             pltpu.VMEM((nx, 8, own_panels), F32),
             pltpu.VMEM((nx, 8, own_panels), F32),
-            pltpu.SemaphoreType.DMA((5 * nx + 6,)),
-            pltpu.SemaphoreType.DMA((5 * nx + 6,)),
+            pltpu.SemaphoreType.DMA((6 * nx + 6,)),
+            pltpu.SemaphoreType.DMA((6 * nx + 6,)),
         ],
         compiler_params=pltpu.CompilerParams(
             collective_id=0, has_side_effects=True, vmem_limit_bytes=48 * 1024 * 1024

time: 108 us -> 106 us (0.981)
  the two profiles are of different devices: /device:TPU:9 before, /device:TPU:0 now
where the time goes in v3:
time: 106 us
  Pallas kernels  98.4 us (93%)
  local copies, waits for them, and re-layouts  6.77 us (6%)
    pallas_call x1, Pallas kernels, body(): pl.pallas_call(functools.partial(tower_kernel, nx, own, dyn), out_shape=(...  98.4 us
    unnamed x9, local copies, waits for them, and re-layouts  5.21 us

profile of v3, /device:TPU:0, one launch (start us, length us, event | category | flops | bytes accessed | tf_op | source)
XLA Modules:
  0.0 105.9 jit_solution(9135717790694994070)
XLA Ops:
  0.6 0.0 copy-start
  0.7 0.8 dynamic_slice.6
  1.4 0.7 pad.4
  2.1 0.0 copy-done
  2.1 0.1 constant_dynamic-slice_fusion
  2.2 0.1 copy.9
  2.3 0.1 fusion.gains
  2.4 0.0 copy-start.1
  2.4 2.2 %copy-done.1 = bf16[1024,2048]{1,0:T(8,128)(2,1)S(1)} copy-done((bf16[1024,2048]{1,0:T(8,128)(2,1)S(1)}, bf16[1024,2048]{1,0:T(8,128)(2,1)}, u32[]{:S(2)}) %copy-start.1) | copy-done | bytes 4194328
  4.6 0.0 copy-start.2
  4.6 0.9 copy-done.2
  5.5 98.4 %shard_map.68 = (bf16[16,4096]{1,0:T(8,128)(2,1)S(1)}, f32[256,512]{1,0:T(8,128)S(1)}) custom-call(bf16[256,512]{1,0:T(8,128)(2,1)S(1)} %bitcast.3, bf16[1024,2048]{1,0:T(8,128)(2,1)S(1)} %copy-done.1, bf16[16,768]{1,0:T(8,128)(2,1)S(1)} %broadcast_in_dim.6.taps, f32[16,64]{1,0:T(8,128)S(1)} %fusion.gains), custom_call_target="tpu_custom_call" | custom-call | tf_op jit(solution)/shard_map/pallas_call | solution.py:433
  104.0 1.3 %copy.8 = f32[256,1,1,512]{3,2,1,0:T(1,128)} copy(f32[256,1,1,512]{3,0,2,1:T(8,128)S(1)} %bitcast.2) | data formatting | bytes 1048576
  105.3 0.7 copy.11
  (1 shorter events, 0.0 us)
Async XLA Ops:
  0.6 1.5 %copy-start = (f32[256,64]{0,1:T(8,128)S(1)}, f32[256,64]{0,1:T(8,128)}, u32[]{:S(2)}) copy-start(f32[256,64]{0,1:T(8,128)} %param.8) | copy-start | bytes 196612
  2.4 2.2 %copy-start.1 = (bf16[1024,2048]{1,0:T(8,128)(2,1)S(1)}, bf16[1024,2048]{1,0:T(8,128)(2,1)}, u32[]{:S(2)}) copy-start(bf16[1024,2048]{1,0:T(8,128)(2,1)} %outside.1) | copy-start | bytes 12582916
  4.6 0.9 copy-start.2

commit v4 on v3

--- a/solution.py
+++ b/solution.py
@@ -137,13 +137,15 @@
 def tower_kernel(
     nx, own, dyn, infl, outside, taps, gains, resp, score, press, fetched,
     lines, raw, from_core, core_sum, from_pair, pair_sum, slots, series, loads, wide_gain,
-    modal, band_back, band_fwd, halo, filt, turned, back, part, arrived, moments, moved,
+    modal, band_back, band_fwd, before, after, tail, filt, turned, back, part, arrived, moments, moved,
     send, recv,
 ):
     rows, panels = press.shape
     modes, own_panels = infl.shape
     total = rows * nx
-    rim = halo.shape[0]
+    rim = before.shape[0]
+    half = panels // 2
+    strip = rim // 2
     spans = total // SPAN
     wind = lax.axis_index("wind")
     gx, gy, gz = lax.axis_index("gx"), lax.axis_index("gy"), lax.axis_index("gz")
@@ -187,7 +189,29 @@
     ]
     for copy in line_copies:
         copy.start()
-    halo_copy = remote(press.at[pl.ds(rows - rim, rim)], halo, extra, {"gx": ahead(1)})
+    up_copies = [
+        remote(
+            press.at[pl.ds(rows - rim + k * strip, strip), pl.ds(0, half)],
+            before.at[pl.ds(k * strip, strip)], extra + 6 + k, {"gx": ahead(1)},
+        )
+        for k in range(2)
+    ]
+    down_copies = [
+        remote(
+            press.at[pl.ds(k * strip, strip), pl.ds(half, half)],
+            after.at[pl.ds(k * strip, strip)], extra + 8 + k, {"gx": behind(1)},
+        )
+        for k in range(2)
+    ]
+
+    def start_strips(k):
+        @pl.when(gx < nx - 1)
+        def _():
+            up_copies[k].start()
+
+        @pl.when(gx > 0)
+        def _():
+            down_copies[k].start()
 
     width = band_back.shape[1]
     reach_to = rim + LEAD
@@ -212,7 +236,11 @@
 
     @pl.when(gx == 0)
     def _():
-        halo[...] = jnp.zeros(halo.shape, BF16)
+        before[...] = jnp.zeros(before.shape, BF16)
+
+    @pl.when(gx == nx - 1)
+    def _():
+        after[...] = jnp.zeros(after.shape, BF16)
 
     def add_lines(block, held, fresh):
         def step(i, _):
@@ -235,6 +263,8 @@
         for o in range(SPAN, rows, SPAN):
             piece = press[pl.ds(o - rim, SPAN + rim), at]
             filt[pl.ds(o, SPAN), at] = dot(band_back[...], piece, ((1,), (0,))).astype(BF16)
+        own_part = dot(band_back[:, pl.ds(rim, SPAN)], press[pl.ds(0, SPAN), at], ((1,), (0,)))
+        filt[pl.ds(0, SPAN), at] = own_part.astype(BF16)
         return 0
 
     lax.fori_loop(0, panels // COLS, filter_later, 0)
@@ -247,9 +277,7 @@
         twin_copies[d - 1].wait_recv()
         add_lines(behind(d), lines.at[d], False)
 
-    @pl.when(gx < nx - 1)
-    def _():
-        halo_copy.start()
+    start_strips(0)
 
     core_copy = remote(raw.at[:, :, 1 - gz], from_core, extra + 1, {"gz": 1 - gz})
     core_copy.start()
@@ -273,6 +301,7 @@
     for d, copy in zip(hops, raw_copies):
         copy.wait_recv()
         series[:, place(behind(d))] = slots[d]
+    start_strips(1)
 
     high, low = [], []
     for i in range(spans):
@@ -355,27 +384,47 @@
 
     @pl.when(gx > 0)
     def _():
-        halo_copy.wait_recv()
+        for copy in up_copies:
+            copy.wait_recv()
+
+    @pl.when(gx < nx - 1)
+    def _():
+        for copy in down_copies:
+            copy.wait_recv()
 
     def filter_first(i, _):
         at = columns(i, COLS)
-        value = dot(band_back[:, pl.ds(0, rim)], halo[:, at], ((1,), (0,)))
-        value += dot(band_back[:, pl.ds(rim, SPAN)], press[pl.ds(0, SPAN), at], ((1,), (0,)))
-        filt[pl.ds(0, SPAN), at] = value.astype(BF16)
+        far = pl.ds(pl.multiple_of(half + i * COLS, COLS), COLS)
+        older = band_back[pl.ds(0, rim), pl.ds(0, rim)]
+        newer = band_back[pl.ds(0, rim), pl.ds(rim, rim)]
+        value = dot(older, before[:, at], ((1,), (0,)))
+        value += dot(newer, press[pl.ds(0, rim), at], ((1,), (0,)))
+        filt[pl.ds(0, rim), at] = value.astype(BF16)
+        value = dot(older, press[pl.ds(rows - rim, rim), far], ((1,), (0,)))
+        value += dot(newer, after[:, at], ((1,), (0,)))
+        tail[:, at] = value.astype(BF16)
         return 0
 
     def measure(block, slot):
+        upper = block >= nx // 2
+        with_first = jnp.where(jnp.logical_or(block < nx // 2, gx == 0), 1.0, 0.0)
+        with_tail = jnp.where(jnp.logical_and(upper, gx < nx - 1), 1.0, 0.0)
+        count = rows - rim + rim * (with_first + with_tail)
         for j in range(own_panels // COLS):
             at = pl.ds(pl.multiple_of(block * own_panels + j * COLS, COLS), COLS)
-            values = filt[:, at].astype(F32)
-            mean = jnp.mean(values, axis=0, keepdims=True)
-            gap = values - mean
+            begin = lax.rem(block, nx // 2) * own_panels + j * COLS
+            pieces = (
+                (1.0, filt[pl.ds(rim, rows - rim), at].astype(F32)),
+                (with_first, filt[pl.ds(0, rim), at].astype(F32)),
+                (with_tail, tail[:, pl.ds(pl.multiple_of(begin, COLS), COLS)].astype(F32)),
+            )
+            mean = sum(w * jnp.sum(v, axis=0, keepdims=True) for w, v in pieces) / count
             moments[slot, pl.ds(0, 1), pl.ds(j * COLS, COLS)] = mean
-            moments[slot, pl.ds(1, 1), pl.ds(j * COLS, COLS)] = jnp.sum(
-                gap * gap, axis=0, keepdims=True
+            moments[slot, pl.ds(1, 1), pl.ds(j * COLS, COLS)] = sum(
+                w * jnp.sum(jnp.square(v - mean), axis=0, keepdims=True) for w, v in pieces
             )
 
-    lax.fori_loop(0, panels // COLS, filter_first, 0)
+    lax.fori_loop(0, half // COLS, filter_first, 0)
     moment_copies = []
     for d in range(nx):
         measure(ahead(d), d)
@@ -388,8 +437,14 @@
         copy.wait_recv()
     means = [moments[0, pl.ds(0, 1), :]] + [moved[d, pl.ds(0, 1), :] for d in hops]
     squares = [moments[0, pl.ds(1, 1), :]] + [moved[d, pl.ds(1, 1), :] for d in hops]
-    mean_panel = sum(means) / nx
-    spread = sum(squares) + rows * sum(jnp.square(m - mean_panel) for m in means)
+    uneven = jnp.where(gx >= nx // 2, 1.0 * rim, 0.0)
+    counts = []
+    for d in range(nx):
+        source = behind(d)
+        sign = jnp.where(source == 0, 1.0, 0.0) - jnp.where(source == nx - 1, 1.0, 0.0)
+        counts.append(rows + uneven * sign)
+    mean_panel = sum(n * m for n, m in zip(counts, means)) / total
+    spread = sum(squares) + sum(n * jnp.square(m - mean_panel) for n, m in zip(counts, means))
     factor = 1.0 / jnp.sqrt(spread / total + 1e-06)
     for copy in cross_copies:
         copy.wait_recv()
@@ -405,7 +460,13 @@
 
     @pl.when(gx < nx - 1)
     def _():
-        halo_copy.wait_send()
+        for copy in up_copies:
+            copy.wait_send()
+
+    @pl.when(gx > 0)
+    def _():
+        for copy in down_copies:
+            copy.wait_send()
 
 
 def body(pressure, fir_taps, influence, mode_impulse, mode_taps):
@@ -417,7 +478,7 @@
     own = modes // (nx * ny * nz)
     own_panels = panels // nx
     dyn = mode_impulse.shape[1]
-    fits = own % 16 == 0 and lax.axis_size("wind") == 2 and modes % 32 == 0 and ny == nz == 2 and rows % SPAN == 0 and own_panels % COLS == 0
+    fits = own % 16 == 0 and lax.axis_size("wind") == 2 and modes % 32 == 0 and ny == nz == 2 and rows % SPAN == 0 and own_panels % COLS == 0 and nx % 2 == 0
     if not fits or rim % LEAD or dyn > LEAD:
         return plain_body(pressure, fir_taps, influence, mode_impulse, mode_taps)
 
@@ -454,7 +515,9 @@
             pltpu.VMEM((own, total + rim), BF16),
             pltpu.VMEM((SPAN, width), BF16),
             pltpu.VMEM((SPAN, width), BF16),
-            pltpu.VMEM((rim, panels), BF16),
+            pltpu.VMEM((rim, panels // 2), BF16),
+            pltpu.VMEM((rim, panels // 2), BF16),
+            pltpu.VMEM((rim, panels // 2), BF16),
             pltpu.VMEM((rows, panels), BF16),
             pltpu.VMEM((nx, own, rows), BF16),
             pltpu.VMEM((nx, 2, 2, own, rows), BF16),
@@ -462,8 +525,8 @@
             pltpu.VMEM((nx, modes, own_panels), BF16),
             pltpu.VMEM((nx, 8, own_panels), F32),
             pltpu.VMEM((nx, 8, own_panels), F32),
-            pltpu.SemaphoreType.DMA((6 * nx + 6,)),
-            pltpu.SemaphoreType.DMA((6 * nx + 6,)),
+            pltpu.SemaphoreType.DMA((6 * nx + 10,)),
+            pltpu.SemaphoreType.DMA((6 * nx + 10,)),
         ],
         compiler_params=pltpu.CompilerParams(
             collective_id=0, has_side_effects=True, vmem_limit_bytes=48 * 1024 * 1024

time: 106 us -> 91.1 us (0.86)
  Pallas kernels: 98.4 us -> 83.2 us
    pallas_call x1, Pallas kernels: 98.4 us -> 83.2 us  [body(): pl.pallas_call(functools.partial(tower_kernel, nx, own, dyn), out_shape=(...]
where the time goes in v4:
time: 91.1 us; the launch traced here: 90.8 us
  Pallas kernels  83.2 us (91%)
  local copies, waits for them, and re-layouts  6.77 us (7%)
    pallas_call x1, Pallas kernels, body(): pl.pallas_call(functools.partial(tower_kernel, nx, own, dyn), out_shape=(...  83.2 us
    unnamed x9, local copies, waits for them, and re-layouts  5.21 us

profile of v4, /device:TPU:0, one launch (start us, length us, event | category | flops | bytes accessed | tf_op | source)
XLA Modules:
  0.0 90.8 jit_solution(17658135826406615296)
XLA Ops:
  0.6 0.0 copy-start
  0.7 0.8 dynamic_slice.6
  1.4 0.7 pad.4
  2.1 0.0 copy-done
  2.1 0.1 constant_dynamic-slice_fusion
  2.2 0.1 copy.9
  2.3 0.1 fusion.gains
  2.4 0.0 copy-start.1
  2.4 2.2 %copy-done.1 = bf16[1024,2048]{1,0:T(8,128)(2,1)S(1)} copy-done((bf16[1024,2048]{1,0:T(8,128)(2,1)S(1)}, bf16[1024,2048]{1,0:T(8,128)(2,1)}, u32[]{:S(2)}) %copy-start.1) | copy-done | bytes 4194328
  4.6 0.0 copy-start.2
  4.6 0.9 %copy-done.2 = bf16[256,1,1,512]{3,0,2,1:T(8,128)(2,1)S(1)} copy-done((bf16[256,1,1,512]{3,0,2,1:T(8,128)(2,1)S(1)}, bf16[256,1,1,512]{3,0,2,1:T(8,128)(2,1)}, u32[]{:S(2)}) %copy-start.2) | copy-done | bytes 262168
  5.5 83.2 %shard_map.68 = (bf16[16,4096]{1,0:T(8,128)(2,1)S(1)}, f32[256,512]{1,0:T(8,128)S(1)}) custom-call(bf16[256,512]{1,0:T(8,128)(2,1)S(1)} %bitcast.3, bf16[1024,2048]{1,0:T(8,128)(2,1)S(1)} %copy-done.1, bf16[16,768]{1,0:T(8,128)(2,1)S(1)} %broadcast_in_dim.6.taps, f32[16,64]{1,0:T(8,128)S(1)} %fusion.gains), custom_call_target="tpu_custom_call" | custom-call | tf_op jit(solution)/shard_map/pallas_call | solution.py:494
  88.8 1.3 %copy.8 = f32[256,1,1,512]{3,2,1,0:T(1,128)} copy(f32[256,1,1,512]{3,0,2,1:T(8,128)S(1)} %bitcast.2) | data formatting | bytes 1048576
  90.1 0.7 copy.11
  (1 shorter events, 0.0 us)
Async XLA Ops:
  0.6 1.5 %copy-start = (f32[256,64]{0,1:T(8,128)S(1)}, f32[256,64]{0,1:T(8,128)}, u32[]{:S(2)}) copy-start(f32[256,64]{0,1:T(8,128)} %param.8) | copy-start | bytes 196612
  2.4 2.2 %copy-start.1 = (bf16[1024,2048]{1,0:T(8,128)(2,1)S(1)}, bf16[1024,2048]{1,0:T(8,128)(2,1)}, u32[]{:S(2)}) copy-start(bf16[1024,2048]{1,0:T(8,128)(2,1)} %outside.1) | copy-start | bytes 12582916
  4.6 0.9 %copy-start.2 = (bf16[256,1,1,512]{3,0,2,1:T(8,128)(2,1)S(1)}, bf16[256,1,1,512]{3,0,2,1:T(8,128)(2,1)}, u32[]{:S(2)}) copy-start(bf16[256,1,1,512]{3,0,2,1:T(8,128)(2,1)} %param.7) | copy-start | bytes 786436

commit v5 on v4

--- a/solution.py
+++ b/solution.py
@@ -279,24 +279,35 @@
 
     start_strips(0)
 
-    core_copy = remote(raw.at[:, :, 1 - gz], from_core, extra + 1, {"gz": 1 - gz})
-    core_copy.start()
-    core_copy.wait_recv()
-    core_sum[...] = raw[:, :, gz] + from_core[...]
-    pair_copy = remote(core_sum.at[:, 1 - gy], from_pair, extra + 2, {"gy": 1 - gy})
-    pair_copy.start()
-    pair_copy.wait_recv()
-    pair_sum[...] = core_sum[:, gy] + from_pair[...]
+    def place(block):
+        return pl.ds(pl.multiple_of(block * rows + rim, LEAD), rows)
+
+    turns = list(hops) + [0]
+    core_base = extra + 10
+    pair_base = core_base + nx
+    core_copies = [
+        remote(raw.at[ahead(d), :, 1 - gz], from_core.at[ahead(d)], core_base + d, {"gz": 1 - gz})
+        for d in turns
+    ]
+    pair_copies = [
+        remote(core_sum.at[ahead(d), 1 - gy], from_pair.at[ahead(d)], pair_base + d, {"gy": 1 - gy})
+        for d in turns
+    ]
     raw_copies = [
         remote(pair_sum.at[ahead(d)], slots.at[d], first["raw"] + d, {"gx": ahead(d)})
         for d in hops
     ]
-    for copy in raw_copies:
+    for copy in core_copies:
         copy.start()
-
-    def place(block):
-        return pl.ds(pl.multiple_of(block * rows + rim, LEAD), rows)
-
+    for i, d in enumerate(turns):
+        core_copies[i].wait_recv()
+        core_sum[ahead(d)] = raw[ahead(d), :, gz] + from_core[ahead(d)]
+        pair_copies[i].start()
+    for i, d in enumerate(turns):
+        pair_copies[i].wait_recv()
+        pair_sum[ahead(d)] = core_sum[ahead(d), gy] + from_pair[ahead(d)]
+        if d:
+            raw_copies[i].start()
     series[:, place(gx)] = pair_sum[gx]
     for d, copy in zip(hops, raw_copies):
         copy.wait_recv()
@@ -354,19 +365,23 @@
         copy.start()
     back[gx, gy, gz] = turned[gx]
 
-    for copy in back_copies:
+    to_pair, to_core, onward = [], [], []
+    spread_base = pair_base + nx
+    for d in range(nx):
+        if d:
+            back_copies[d - 1].wait_recv()
+        mine = back.at[behind(d), gy, gz]
+        to_pair.append(remote(mine, mine, spread_base + d, {"gy": 1 - gy}))
+        to_core.append(remote(mine, mine, spread_base + nx + d, {"gz": 1 - gz}))
+        to_pair[d].start()
+        to_core[d].start()
+    for d in range(nx):
+        to_pair[d].wait_recv()
+        other = back.at[behind(d), 1 - gy, gz]
+        onward.append(remote(other, other, spread_base + 2 * nx + d, {"gz": 1 - gz}))
+        onward[d].start()
+    for copy in to_core + onward:
         copy.wait_recv()
-    mine = back.at[:, gy, gz]
-    back_pair = remote(mine, mine, extra + 3, {"gy": 1 - gy})
-    back_core = remote(mine, mine, extra + 4, {"gz": 1 - gz})
-    back_pair.start()
-    back_core.start()
-    back_pair.wait_recv()
-    other = back.at[:, 1 - gy, gz]
-    back_forward = remote(other, other, extra + 5, {"gz": 1 - gz})
-    back_forward.start()
-    back_core.wait_recv()
-    back_forward.wait_recv()
 
     def cross_block(block, j):
         at = pl.ds(pl.multiple_of(block * own_panels + j * COLS, COLS), COLS)
@@ -455,7 +470,7 @@
 
     for copy in line_copies + twin_copies + raw_copies + back_copies + moment_copies + cross_copies:
         copy.wait_send()
-    for copy in (core_copy, pair_copy, back_pair, back_core, back_forward):
+    for copy in core_copies + pair_copies + to_pair + to_core + onward:
         copy.wait_send()
 
     @pl.when(gx < nx - 1)
@@ -525,8 +540,8 @@
             pltpu.VMEM((nx, modes, own_panels), BF16),
             pltpu.VMEM((nx, 8, own_panels), F32),
             pltpu.VMEM((nx, 8, own_panels), F32),
-            pltpu.SemaphoreType.DMA((6 * nx + 10,)),
-            pltpu.SemaphoreType.DMA((6 * nx + 10,)),
+            pltpu.SemaphoreType.DMA((11 * nx + 10,)),
+            pltpu.SemaphoreType.DMA((11 * nx + 10,)),
         ],
         compiler_params=pltpu.CompilerParams(
             collective_id=0, has_side_effects=True, vmem_limit_bytes=48 * 1024 * 1024

time: 91.1 us -> 88.4 us (0.970)
  Pallas kernels: 83.2 us -> 80.6 us
    pallas_call x1, Pallas kernels: 83.2 us -> 80.6 us  [body(): pl.pallas_call(functools.partial(tower_kernel, nx, own, dyn), out_shape=(...]
where the time goes in v5:
time: 88.4 us; the launch traced here: 88.1 us
  Pallas kernels  80.6 us (91%)
  local copies, waits for them, and re-layouts  6.77 us (8%)
    pallas_call x1, Pallas kernels, body(): pl.pallas_call(functools.partial(tower_kernel, nx, own, dyn), out_shape=(...  80.6 us
    unnamed x9, local copies, waits for them, and re-layouts  5.21 us

profile of v5, /device:TPU:0, one launch (start us, length us, event | category | flops | bytes accessed | tf_op | source)
XLA Modules:
  0.0 88.1 jit_solution(5027683369230818398)
XLA Ops:
  0.6 0.0 copy-start
  0.7 0.8 dynamic_slice.6
  1.4 0.7 pad.4
  2.1 0.0 copy-done
  2.1 0.1 constant_dynamic-slice_fusion
  2.2 0.1 copy.9
  2.3 0.1 fusion.gains
  2.4 0.0 copy-start.1
  2.4 2.2 %copy-done.1 = bf16[1024,2048]{1,0:T(8,128)(2,1)S(1)} copy-done((bf16[1024,2048]{1,0:T(8,128)(2,1)S(1)}, bf16[1024,2048]{1,0:T(8,128)(2,1)}, u32[]{:S(2)}) %copy-start.1) | copy-done | bytes 4194328
  4.6 0.0 copy-start.2
  4.6 0.9 %copy-done.2 = bf16[256,1,1,512]{3,0,2,1:T(8,128)(2,1)S(1)} copy-done((bf16[256,1,1,512]{3,0,2,1:T(8,128)(2,1)S(1)}, bf16[256,1,1,512]{3,0,2,1:T(8,128)(2,1)}, u32[]{:S(2)}) %copy-start.2) | copy-done | bytes 262168
  5.5 80.6 %shard_map.68 = (bf16[16,4096]{1,0:T(8,128)(2,1)S(1)}, f32[256,512]{1,0:T(8,128)S(1)}) custom-call(bf16[256,512]{1,0:T(8,128)(2,1)S(1)} %bitcast.3, bf16[1024,2048]{1,0:T(8,128)(2,1)S(1)} %copy-done.1, bf16[16,768]{1,0:T(8,128)(2,1)S(1)} %broadcast_in_dim.6.taps, f32[16,64]{1,0:T(8,128)S(1)} %fusion.gains), custom_call_target="tpu_custom_call" | custom-call | tf_op jit(solution)/shard_map/pallas_call | solution.py:509
  86.1 1.3 %copy.8 = f32[256,1,1,512]{3,2,1,0:T(1,128)} copy(f32[256,1,1,512]{3,0,2,1:T(8,128)S(1)} %bitcast.2) | data formatting | bytes 1048576
  87.5 0.7 copy.11
  (1 shorter events, 0.0 us)
Async XLA Ops:
  0.6 1.5 %copy-start = (f32[256,64]{0,1:T(8,128)S(1)}, f32[256,64]{0,1:T(8,128)}, u32[]{:S(2)}) copy-start(f32[256,64]{0,1:T(8,128)} %param.8) | copy-start | bytes 196612
  2.4 2.2 %copy-start.1 = (bf16[1024,2048]{1,0:T(8,128)(2,1)S(1)}, bf16[1024,2048]{1,0:T(8,128)(2,1)}, u32[]{:S(2)}) copy-start(bf16[1024,2048]{1,0:T(8,128)(2,1)} %outside.1) | copy-start | bytes 12582916
  4.6 0.9 %copy-start.2 = (bf16[256,1,1,512]{3,0,2,1:T(8,128)(2,1)S(1)}, bf16[256,1,1,512]{3,0,2,1:T(8,128)(2,1)}, u32[]{:S(2)}) copy-start(bf16[256,1,1,512]{3,0,2,1:T(8,128)(2,1)} %param.7) | copy-start | bytes 786436
